TPU v7x, 256 devices: a whole 4x4x8 slice. The times are simulated.
256 devices in a mesh: scen: 8 (over z_lo, y), obl: 32 (over z_hi, x, core).
Axes of the slice: x: 4, y: 4, z: 8 (z_hi: 4, z_lo: 2; z = z_hi * 2 + z_lo), core: 2. Of those that a mesh axis runs over, the one named last changes fastest.
Arguments:
- factor_draws: bfloat16 [16384, 128], P(('scen', 'obl')), may hold values from -5 to 5
- loadings: bfloat16 [131072, 128], P(('scen', 'obl')), may hold values from -0.45 to 0.5
- sector: int32 [131072], P(('scen', 'obl')), may hold values from 0 to 11
- threshold: bfloat16 [131072], P(('scen', 'obl')), may hold values from -3.59375 to -2.796875
- idio: bfloat16 [131072], P(('scen', 'obl')), may hold values from 0.59765625 to 1
- exposure: bfloat16 [131072], P(('scen', 'obl')), may hold values from 0.19921875 to 1
- theta: float32 [1], replicated, may hold values from 1 to 2
Outputs:
- relative_weights: float32 [16384], P(('scen', 'obl'))
- sensitivities: float32 [131072, 128], P(('scen', 'obl'))
All inputs are finite; a program needn't handle non-finite values.
Results may differ from a plain program's by a relative error of at most 0.0035.
Values may be sent and summed in bfloat16 or wider, within the bound.
A program may use at most 64 MiB of HBM per device.

v0:
```python
import math

import jax
import jax.numpy as jnp
from jax import lax
from jax.sharding import PartitionSpec as P

FACTORS = 128
GLOBAL_F = 32
SECTOR_F = 8


ROOT_HALF = 0.7071067811865476
NORMAL_PEAK = 0.3989422804014327
SCALE_OUT = 300.0


def sector_mask(sector):
    column_ids = lax.broadcasted_iota(jnp.int32, (sector.shape[0], FACTORS), 1)
    in_block = (column_ids - GLOBAL_F) // SECTOR_F == sector[:, None]
    return (column_ids < GLOBAL_F) | in_block


def obligor_terms(scores, limits, spreads, amounts, twist):
    shifted = (limits[None, :] + scores) / spreads[None, :]
    prob = 0.5 * jax.scipy.special.erfc(-shifted * ROOT_HALF)
    growth = jnp.exp(twist * amounts)[None, :]
    denom = 1.0 + prob * (growth - 1.0)
    twisted = prob * growth / denom
    return (shifted, growth, denom, twisted)


def obligor_pieces(rows, threshold, idio, exposure):
    obl_total = rows.shape[0]
    obl_block = math.gcd(obl_total, 2048)
    obl_count = obl_total // obl_block
    return (
        rows.reshape(obl_count, obl_block, rows.shape[1]),
        threshold.astype(jnp.float32).reshape(obl_count, obl_block),
        idio.astype(jnp.float32).reshape(obl_count, obl_block),
        exposure.astype(jnp.float32).reshape(obl_count, obl_block),
    )


def row_sums(draws, rows, threshold, idio, exposure, twist):
    scen_total = draws.shape[0]
    scen_block = math.gcd(scen_total, 512)
    pieces = obligor_pieces(rows, threshold, idio, exposure)

    def row_per_block(draw_block):

        def row_step(carry, piece):
            block_rows, limits, spreads, amounts = piece
            scores = lax.dot_general(
                draw_block, block_rows, (((1,), (1,)), ((), ())), preferred_element_type=jnp.float32
            )
            shifted, growth, denom, twisted = obligor_terms(scores, limits, spreads, amounts, twist)
            return (
                (
                    carry[0] + jnp.sum(jnp.log(denom), axis=1),
                    carry[1] + jnp.sum(amounts[None, :] * twisted, axis=1),
                ),
                None,
            )

        zeros_row = jnp.zeros((draw_block.shape[0],), jnp.float32)
        sums, unused = lax.scan(row_step, (zeros_row, zeros_row), pieces)
        return sums

    cumulant, twisted_loss = lax.map(
        row_per_block, draws.reshape(scen_total // scen_block, scen_block, draws.shape[1])
    )
    return (cumulant.reshape(scen_total), twisted_loss.reshape(scen_total))


def grad_rows(draws, weights, rows, threshold, idio, exposure, twist):
    scen_total = draws.shape[0]
    scen_block = math.gcd(scen_total, 512)
    scen_count = scen_total // scen_block
    scen_pieces = (
        draws.reshape(scen_count, scen_block, draws.shape[1]),
        weights.reshape(scen_count, scen_block),
    )
    pieces = obligor_pieces(rows, threshold, idio, exposure)

    def grad_per_block(piece):
        block_rows, limits, spreads, amounts = piece

        def grad_step(carry, part):
            draw_block, weight_block = part
            scores = lax.dot_general(
                draw_block, block_rows, (((1,), (1,)), ((), ())), preferred_element_type=jnp.float32
            )
            shifted, growth, denom, twisted = obligor_terms(scores, limits, spreads, amounts, twist)
            slope = (
                SCALE_OUT
                * weight_block[:, None]
                * amounts[None, :]
                * growth
                / (denom * denom)
                * NORMAL_PEAK
                * jnp.exp(-0.5 * shifted * shifted)
                / spreads[None, :]
            ).astype(jnp.bfloat16)
            update = lax.dot_general(
                slope, draw_block, (((0,), (0,)), ((), ())), preferred_element_type=jnp.float32
            )
            return (carry + update, None)

        zeros_block = jnp.zeros((block_rows.shape[0], draws.shape[1]), jnp.float32)
        result, unused = lax.scan(grad_step, zeros_block, scen_pieces)
        return result

    return lax.map(grad_per_block, pieces).reshape(rows.shape[0], draws.shape[1])


def shards(factor_draws, loadings, sector, threshold, idio, exposure, theta):
    twist = theta[0]
    mask = sector_mask(sector)
    active = jnp.where(mask, loadings, jnp.zeros_like(loadings))
    draws = lax.all_gather(factor_draws, ("scen", "obl"), axis=0, tiled=True)
    cumulant, twisted_loss = row_sums(draws, active, threshold, idio, exposure, twist)
    cumulant, twisted_loss = lax.psum((cumulant, twisted_loss), ("scen", "obl"))
    logit = cumulant - twist * twisted_loss
    top = jnp.max(logit)
    unnormed = jnp.exp(logit - top)
    weights = unnormed / jnp.sum(unnormed)
    sensitivity = grad_rows(draws, weights, active, threshold, idio, exposure, twist)
    offset = lax.axis_index(("scen", "obl")) * factor_draws.shape[0]
    count_all = draws.shape[0]
    own_weights = lax.dynamic_slice_in_dim(weights, offset, factor_draws.shape[0])
    return (count_all * own_weights, jnp.where(mask, sensitivity, 0.0))


def solution(mesh):
    return jax.shard_map(
        shards,
        mesh=mesh,
        in_specs=(
            P(("scen", "obl"), None),
            P(("scen", "obl"), None),
            P(("scen", "obl")),
            P(("scen", "obl")),
            P(("scen", "obl")),
            P(("scen", "obl")),
            P(),
        ),
        out_specs=(P(("scen", "obl")), P(("scen", "obl"), None)),
        check_vma=False,
    )
```

profile of v0, /device:TPU:1, one launch (start us, length us, event | category | flops | bytes accessed | tf_op | source)
XLA Modules:
  0.0 994.3 jit_solution(12083805725722403885)
XLA Ops:
  11.1 415.7 %all-gather.2.cloned.1.call-done = bf16[16384,128]{1,0:T(8,128)(2,1)} async-done(((bf16[64,128]{1,0:T(8,128)(2,1)}), bf16[16384,128]{1,0:T(8,128)(2,1)}) %all-gather.2.cloned.1.call-update) | async-done | bytes 4194320 | tf_op jit(solution)/shard_map/all_gather | solution.py:121
  426.8 156.3 %while.39 = (s32[]{:T(128)}, f32[32,512]{1,0:T(8,128)S(1)}, f32[32,512]{1,0:T(8,128)S(1)}, f32[1,512]{1,0:T(1,128)S(1)}, bf16[32,512,128]{2,1,0:T(8,128)(2,1)}, ...) while((s32[]{:T(128)}, f32[32,512]{1,0:T(8,128)S(1)}, ...), condition=%wide.region_3.4_spmd, body=%wide.region_0.3_spmd.sunk | while | flops 85722112 | bytes 290949 | solution.py:70
  585.3 238.8 %all-reduce.3.cloned.1.call-done = (f32[16384]{0:T(1024)}, f32[16384]{0:T(1024)}) async-done(((f32[16384]{0:T(1024)}, f32[16384]{0:T(1024)}), (f32[16384]{0:T(1024)}, f32[16384]{0:T(1024)})) %all-reduce.3.cloned.1.call-update) | async-done | bytes 131088 | tf_op jit(solution)/shard_map/psum | solution.py:123
  828.7 157.9 %while.40 = (s32[]{:T(128)}, f32[512,128]{1,0:T(8,128)S(1)}, f32[32,512]{1,0:T(8,128)S(1)}, f32[512]{0:T(512)S(1)}, f32[]{:T(128)}, /*index=5*/f32[512]{0:T(512)...) while((s32[]{:T(128)}, f32[512,128]{1,0:T(8,128)S(1)}, ...), condition=%wide.region_9.10_spmd.clone, body=%wide.region_8.9_spmd.clone.sunk | while | flops 154273792 | bytes 941702 | solution.py:111
  829.4 4.2 convolution_add_fusion.4
  834.3 4.2 convolution_add_fusion.4
  839.3 4.2 convolution_add_fusion.4
  844.2 4.2 convolution_add_fusion.4
  849.1 4.2 convolution_add_fusion.4
  854.1 4.2 convolution_add_fusion.4
  859.0 4.2 convolution_add_fusion.4
  863.9 4.2 convolution_add_fusion.4
  868.9 4.2 convolution_add_fusion.4
  873.8 4.2 convolution_add_fusion.4
  878.7 4.2 convolution_add_fusion.4
  888.6 4.2 convolution_add_fusion.4
  893.5 4.2 convolution_add_fusion.4
  898.5 4.2 convolution_add_fusion.4
  903.4 4.2 convolution_add_fusion.4
  908.3 4.2 convolution_add_fusion.4
  913.3 4.2 convolution_add_fusion.4
  918.2 4.2 convolution_add_fusion.4
  923.2 4.2 convolution_add_fusion.4
  928.1 4.2 convolution_add_fusion.4
  (230 shorter events, 237.8 us)
Async XLA Ops:
  7.2 419.6 %all-gather.2.cloned.1.call-start = ((), (), s32[]{:S(2)}) async-start(), calls=%async_computation | async-start | bytes 4210688 | tf_op jit(solution)/shard_map/all_gather | solution.py:121
  7.9 816.1 %all-reduce.3.cloned.1.call-start = ((), (), s32[]{:S(2)}) async-start(), calls=%async_computation.1 | async-start | bytes 262144 | tf_op jit(solution)/shard_map/psum | solution.py:123
  426.8 157.6 %copy-start = (bf16[512,128]{1,0:T(8,128)(2,1)S(1)}, bf16[512,128]{1,0:T(8,128)(2,1)}, u32[]{:S(2)}) copy-start(bf16[512,128]{1,0:T(8,128)(2,1)} %param.12) | copy-start | bytes 393220
  426.8 157.6 %copy-start.1 = (s32[512]{0:T(512)S(1)}, s32[512]{0:T(512)}, u32[]{:S(2)}) copy-start(s32[512]{0:T(512)} %param.13) | copy-start | bytes 6148
Sparse Core Ops, SparseCore 0:
  9.9 416.8 all-gather.1
  584.5 239.4 all-reduce.2
where the time goes:
time: 996 us; the launch traced here: 994 us
  waiting for transfers between devices  655 us (66%)
  matrix products  265 us (27%)
  other arithmetic  51 us (5%)
  between operations  14.8 us (1%)
    all_gather x1, waiting for transfers between devices, shards(): draws = lax.all_gather(factor_draws, ('scen', 'obl'), axis=0, tiled=True)  416 us
    psum x1, waiting for transfers between devices, shards(): cumulant, twisted_loss = lax.psum((cumulant, twisted_loss), ('scen', 'obl'))  239 us
    dot_general x32, matrix products, grad_step(): lax.dot_general(slope, draw_block, (((0,), (0,)), ((), ())), preferred_el...  135 us
    dot_general x32, matrix products, row_step(): lax.dot_general(draw_block, block_rows, (((1,), (1,)), ((), ())), preferr...  130 us
    mul x64, other arithmetic, obligor_terms(): denom = 1.0 + prob * (growth - 1.0)  41.9 us
  transfers between devices with their start and end apart: 2, of which 2 were waited for; matrix products, arithmetic and copies ran while one was open for 0% of the time, Pallas kernels for 0%

commit v1 on v0

v1 whole, which is shorter than its diff:
```python
import functools

import jax
import jax.numpy as jnp
from jax import lax
from jax.experimental import pallas as pl
from jax.experimental.pallas import tpu as pltpu
from jax.sharding import PartitionSpec as P

F32 = jnp.float32
BF16 = jnp.bfloat16
MESH = pl.DeviceIdType.MESH
LANES = 128
FACTORS = 128
GLOBAL_F = 32
SECTOR_F = 8
SIDE = 4
DEPTH = 8
OWN = 64
UNIT = DEPTH * OWN
HALF = SIDE * SIDE * UNIT
SCENARIOS = 2 * HALF
UNITS = SCENARIOS // UNIT
OBL = 512
ROWS = 128
GROUP = 64
STRETCH = 256
PEERS = SIDE * SIDE
ROOT_HALF = 0.7071067811865476
NORMAL_PEAK = 0.3989422804014327
SCALE_OUT = 300.0
LOG2_E = 1.4426950408889634
NT = (((1,), (1,)), ((), ()))


def place():
    scen, obl = lax.axis_index("scen"), lax.axis_index("obl")
    z = (obl // 8) * 2 + scen // 4
    return (obl // 2) % 4, scen % 4, z, obl % 2


def device(x, y, z, core):
    return ((z % 2) * 4 + y, (z // 2) * 8 + x * 2 + core)


def columns(row):
    return jnp.transpose(jnp.broadcast_to(row, (LANES, LANES)))


def wide(value):
    return jnp.concatenate([value] * (UNIT // LANES), axis=1)


def kernel(
    draws_ref,
    load_ref,
    sector_ref,
    threshold_ref,
    idio_ref,
    exposure_ref,
    theta_ref,
    weight_ref,
    sens_ref,
    draws,
    slopes,
    active,
    inverse,
    offset,
    shift,
    gain,
    centre,
    level,
    scale,
    logit,
    total,
    part1,
    part2,
    send1,
    recv1,
    send2,
    recv2,
    send3,
    recv3,
    send_f,
    recv_f,
    send_r,
    recv_r,
):
    x, y, z, core = place()
    p1 = y + core * (x - y)
    p2 = x + core * (y - x)

    def along1(step):
        q = (p1 + step) % SIDE
        return device(x + core * (q - x), y + (1 - core) * (q - y), z, core)

    def along2(step):
        q = (p2 + step) % SIDE
        return device(x + (1 - core) * (q - x), y + core * (q - y), z, core)

    partner = device(x, y, z, 1 - core)
    plane = x * SIDE + y
    stack = z * 2 + core

    def plane_peer(j):
        return device(j // SIDE, j % SIDE, z, core)

    def stack_peer(j):
        return device(x, y, j // 2, j % 2)

    barrier = pltpu.get_barrier_semaphore()
    for step in range(1, PEERS):
        for peer in (plane_peer((plane + step) % PEERS), stack_peer((stack + step) % PEERS)):
            pl.semaphore_signal(barrier, inc=1, device_id=peer, device_id_type=MESH)
    pl.semaphore_wait(barrier, 2 * (PEERS - 1))

    def unit_index(half, a, b):
        return half * PEERS + a * SIDE + b

    def unit_rows(index):
        return pl.ds(pl.multiple_of(index * UNIT, UNIT), UNIT)

    def own_index(d, e):
        return unit_index(core, (p2 + SIDE - d) % SIDE, (p1 + SIDE - e) % SIDE)

    def partner_index(d, e):
        return unit_index(1 - core, (p1 + SIDE - d) % SIDE, (p2 + SIDE - e) % SIDE)

    def copy1(step, from_z):
        rows = pl.ds(pl.multiple_of(own_index(0, 0) * UNIT + from_z * OWN, OWN), OWN)
        return pltpu.make_async_remote_copy(
            src_ref=draws_ref,
            dst_ref=draws.at[rows],
            send_sem=send1.at[step],
            recv_sem=recv1.at[step],
            device_id=device(x, y, (z + step) % DEPTH, core),
            device_id_type=MESH,
        )

    def unit_copy(index, send, recv, peer):
        rows = unit_rows(index)
        return pltpu.make_async_remote_copy(
            src_ref=draws.at[rows],
            dst_ref=draws.at[rows],
            send_sem=send,
            recv_sem=recv,
            device_id=peer,
            device_id_type=MESH,
        )

    def copy2(step, e):
        return unit_copy(own_index(0, e), send2.at[step], recv2.at[step], along1(step))

    def copy3(e, step, d):
        return unit_copy(own_index(d, e), send3.at[e, step], recv3.at[e, step], along2(step))

    def forward(d, e, index):
        return unit_copy(index, send_f.at[d, e], recv_f.at[d, e], partner)

    for step in range(1, DEPTH):
        copy1(step, z).start()
    mine = pl.ds(pl.multiple_of(own_index(0, 0) * UNIT + z * OWN, OWN), OWN)
    draws[mine, :] = draws_ref[...]

    twist = theta_ref[0]
    ids = lax.broadcasted_iota(jnp.int32, (LANES, FACTORS), 1)
    for block in range(OBL // LANES):
        rows = pl.ds(block * LANES, LANES)
        one = pl.ds(block, 1)
        idio = idio_ref[one, :].astype(F32)
        amount = exposure_ref[one, :].astype(F32)
        limit = threshold_ref[one, :].astype(F32)
        growth = jnp.exp(twist * amount)
        half = 0.5 * (growth - 1.0)
        spread = ROOT_HALF / idio
        costs = twist * amount * growth / (growth - 1.0)
        inverse[rows, :] = columns(spread)
        offset[rows, :] = columns(limit * spread)
        shift[rows, :] = columns(1.0 / half + 1.0)
        gain[rows, :] = columns(costs / half)
        scale[rows, :] = columns(
            (SCALE_OUT * NORMAL_PEAK) * amount * growth / (idio * half * half)
        )
        full_cost = columns(costs)
        for group in range(LANES // GROUP):
            part = full_cost[group * GROUP : (group + 1) * GROUP]
            centre[pl.ds((block * LANES // GROUP + group) * 8, 8), :] = jnp.sum(
                part.reshape(GROUP // 8, 8, LANES), axis=0
            )
        full_half = columns(half).reshape(LANES // 8, 8, LANES)
        product = full_half[0]
        for k in range(1, LANES // 8):
            product = product * full_half[k]
        at = pl.ds((block * LANES // STRETCH) * 8, 8)
        if (block * LANES) % STRETCH == 0:
            level[at, :] = product
        else:
            level[at, :] = level[at, :] * product
        sector = columns(sector_ref[one, :].astype(F32)).astype(jnp.int32)
        first = GLOBAL_F + sector * SECTOR_F
        mask = (ids < GLOBAL_F) | ((ids >= first) & (ids < first + SECTOR_F))
        active[rows, :] = jnp.where(mask, load_ref[rows, :].astype(F32), 0.0).astype(BF16)
        scale[rows, :] = jnp.where(mask, scale[rows, :], 0.0)

    def compute(index):
        draw_rows = draws[unit_rows(index), :]
        lanes = pl.ds(pl.multiple_of(index * UNIT, UNIT), UNIT)
        acc = jnp.zeros((8, UNIT), F32)
        product = None
        for r in range(0, OBL, ROWS):
            rows = pl.ds(r, ROWS)
            score = lax.dot_general(active[rows, :], draw_rows, NT, preferred_element_type=F32)
            arg = score * wide(inverse[rows, :]) + wide(offset[rows, :])
            denom = lax.erf(arg) + wide(shift[rows, :])
            share = pl.reciprocal(denom)
            slopes[rows, lanes] = (jnp.exp2((arg * arg) * -LOG2_E) * share * share).astype(BF16)
            loss = share * wide(gain[rows, :])
            if r % STRETCH == 0:
                product = denom[:8]
            for k in range(0 if r % STRETCH else 1, ROWS // 8):
                product = product * denom[k * 8 : k * 8 + 8]
            for g in range(0, ROWS, GROUP):
                some = loss[g : g + 8]
                for k in range(1, GROUP // 8):
                    some = some + loss[g + k * 8 : g + k * 8 + 8]
                acc = acc + (some - wide(centre[pl.ds((r + g) // GROUP * 8, 8), :]))
            if (r + ROWS) % STRETCH == 0:
                acc = acc + jnp.log(product * wide(level[pl.ds(r // STRETCH * 8, 8), :]))
        logit[pl.ds(index, 1), :] = jnp.sum(acc, axis=0, keepdims=True)

    for step in range(1, DEPTH):
        copy1(step, (z + DEPTH - step) % DEPTH).wait_recv()
    for step in range(1, SIDE):
        copy2(step, 0).start()

    def turn(n, carry):
        group, e = n // SIDE, n % SIDE
        d = group + (group // 2) * (5 - 2 * group)

        @pl.when((n > 0) & (n < SIDE))
        def _():
            copy2(e, e).wait_recv()

        @pl.when(n >= SIDE)
        def _():
            copy3(e, d, d).wait_recv()

        @pl.when(n < SIDE)
        def _():
            for step in range(1, SIDE):
                copy3(e, step, 0).start()

        forward(d, e, own_index(d, e)).start()

        def side(which, carry):
            @pl.when(which == 1)
            def _():
                forward(d, e, partner_index(d, e)).wait_recv()

            compute(own_index(d, e) + which * (partner_index(d, e) - own_index(d, e)))
            return carry

        return lax.fori_loop(0, 2, side, carry)

    lax.fori_loop(0, UNITS // 2, turn, 0)

    def tile(j):
        return (
            pl.ds(pl.multiple_of(j // SIDE * 8, 8), 8),
            pl.ds(pl.multiple_of(j % SIDE * LANES, LANES), LANES),
        )

    def reduce1(step, j, peer):
        return pltpu.make_async_remote_copy(
            src_ref=logit.at[tile(j)],
            dst_ref=part1.at[plane],
            send_sem=send_r.at[0, step],
            recv_sem=recv_r.at[0, step],
            device_id=peer,
            device_id_type=MESH,
        )

    def reduce2(step, peer):
        return pltpu.make_async_remote_copy(
            src_ref=part2.at[stack],
            dst_ref=part2.at[stack],
            send_sem=send_r.at[1, step],
            recv_sem=recv_r.at[1, step],
            device_id=peer,
            device_id_type=MESH,
        )

    def reduce3(step, peer):
        return pltpu.make_async_remote_copy(
            src_ref=total.at[tile(plane)],
            dst_ref=total.at[tile(plane)],
            send_sem=send_r.at[2, step],
            recv_sem=recv_r.at[2, step],
            device_id=peer,
            device_id_type=MESH,
        )

    def arrival1(step):
        j = (plane + PEERS - step) % PEERS
        return pltpu.make_async_remote_copy(
            src_ref=logit.at[tile(plane)],
            dst_ref=part1.at[j],
            send_sem=send_r.at[0, step],
            recv_sem=recv_r.at[0, step],
            device_id=plane_peer(j),
            device_id_type=MESH,
        )

    def arrival2(step):
        j = (stack + PEERS - step) % PEERS
        return pltpu.make_async_remote_copy(
            src_ref=part2.at[stack],
            dst_ref=part2.at[j],
            send_sem=send_r.at[1, step],
            recv_sem=recv_r.at[1, step],
            device_id=stack_peer(j),
            device_id_type=MESH,
        )

    def arrival3(step):
        j = (plane + PEERS - step) % PEERS
        return pltpu.make_async_remote_copy(
            src_ref=total.at[tile(plane)],
            dst_ref=total.at[tile(j)],
            send_sem=send_r.at[2, step],
            recv_sem=recv_r.at[2, step],
            device_id=plane_peer(j),
            device_id_type=MESH,
        )

    def to_plane(step):
        j = (plane + step) % PEERS
        return reduce1(step, j, plane_peer(j))

    def to_stack(step):
        return reduce2(step, stack_peer((stack + step) % PEERS))

    def back_to_plane(step):
        return reduce3(step, plane_peer((plane + step) % PEERS))

    for step in range(1, PEERS):
        to_plane(step).start()
    part1[plane] = logit[tile(plane)]
    for step in range(1, PEERS):
        arrival1(step).wait_recv()
    part2[stack] = jnp.sum(part1[...], axis=0)
    for step in range(1, PEERS):
        to_stack(step).start()
    for step in range(1, PEERS):
        arrival2(step).wait_recv()
    total[tile(plane)] = jnp.sum(part2[...], axis=0)
    for step in range(1, PEERS):
        back_to_plane(step).start()

    for step in range(1, DEPTH):
        copy1(step, z).wait_send()
    for step in range(1, SIDE):
        copy2(step, 0).wait_send()
        for e in range(SIDE):
            copy3(e, step, 0).wait_send()
    for d in range(SIDE):
        for e in range(SIDE):
            forward(d, e, own_index(d, e)).wait_send()
    for step in range(1, PEERS):
        to_plane(step).wait_send()
        to_stack(step).wait_send()
    for step in range(1, PEERS):
        arrival3(step).wait_recv()
    for step in range(1, PEERS):
        back_to_plane(step).wait_send()

    logits = total[...]
    raw = jnp.exp(logits - jnp.max(logits))
    norm = 1.0 / jnp.sum(raw)
    total[...] = raw
    own_row = total[pl.ds(own_index(0, 0), 1), :]
    own = jnp.zeros((1, OWN), F32)
    for k in range(DEPTH):
        own = jnp.where(z == k, own_row[:, k * OWN : (k + 1) * OWN], own)
    weight_ref[...] = own * (norm * SCENARIOS)

    for j in range(UNIT // LANES):
        turned = jnp.transpose(raw[:, j * LANES : (j + 1) * LANES])
        for u in range(UNITS):
            rows = pl.ds(u * UNIT + j * LANES, LANES)
            draws[rows, :] = (draws[rows, :].astype(F32) * turned[:, u : u + 1]).astype(BF16)

    sens_ref[...] = jnp.zeros_like(sens_ref)
    depth = 2 * UNIT

    def add(n, carry):
        at = pl.ds(pl.multiple_of(n * depth, depth), depth)
        sens_ref[...] += jnp.dot(slopes[:, at], draws[at, :], preferred_element_type=F32)
        return carry

    lax.fori_loop(0, SCENARIOS // depth, add, 0)
    sens_ref[...] = sens_ref[...] * (scale[...] * norm)


def shards(factor_draws, loadings, sector, threshold, idio, exposure, theta):
    rows = OBL // LANES
    vmem = pl.BlockSpec(memory_space=pltpu.VMEM)
    constant = pltpu.VMEM((OBL, LANES), F32)
    dma = pltpu.SemaphoreType.DMA
    weights, sensitivities = pl.pallas_call(
        kernel,
        out_shape=[
            jax.ShapeDtypeStruct((1, OWN), F32),
            jax.ShapeDtypeStruct((OBL, FACTORS), F32),
        ],
        in_specs=[vmem] * 6 + [pl.BlockSpec(memory_space=pltpu.SMEM)],
        out_specs=[vmem] * 2,
        scratch_shapes=[
            pltpu.VMEM((SCENARIOS, FACTORS), BF16),
            pltpu.VMEM((OBL, SCENARIOS), BF16),
            pltpu.VMEM((OBL, FACTORS), BF16),
            constant,
            constant,
            constant,
            constant,
            pltpu.VMEM((OBL // GROUP * 8, LANES), F32),
            pltpu.VMEM((OBL // STRETCH * 8, LANES), F32),
            constant,
            pltpu.VMEM((UNITS, UNIT), F32),
            pltpu.VMEM((UNITS, UNIT), F32),
            pltpu.VMEM((PEERS, 8, LANES), F32),
            pltpu.VMEM((PEERS, 8, LANES), F32),
            dma((DEPTH,)),
            dma((DEPTH,)),
            dma((SIDE,)),
            dma((SIDE,)),
            dma((SIDE, SIDE)),
            dma((SIDE, SIDE)),
            dma((SIDE, SIDE)),
            dma((SIDE, SIDE)),
            dma((3, PEERS)),
            dma((3, PEERS)),
        ],
        compiler_params=pltpu.CompilerParams(
            collective_id=0, has_side_effects=True, vmem_limit_bytes=56 << 20
        ),
    )(
        factor_draws,
        loadings,
        sector.reshape(rows, LANES),
        threshold.reshape(rows, LANES),
        idio.reshape(rows, LANES),
        exposure.reshape(rows, LANES),
        theta,
    )
    return weights.reshape(OWN), sensitivities


def solution(mesh):
    return jax.shard_map(
        shards,
        mesh=mesh,
        in_specs=(
            P(("scen", "obl"), None),
            P(("scen", "obl"), None),
            P(("scen", "obl")),
            P(("scen", "obl")),
            P(("scen", "obl")),
            P(("scen", "obl")),
            P(),
        ),
        out_specs=(P(("scen", "obl")), P(("scen", "obl"), None)),
        check_vma=False,
    )
```

time: 996 us -> 83 us (0.08)
  waiting for transfers between devices: 655 us -> 0 us
  matrix products: 265 us -> 0 us
  Pallas kernels: 0 us -> 78.8 us
  other arithmetic: 51 us -> 0 us
  between operations: 14.8 us -> 1.3 us
    all_gather x1 -> x0, waiting for transfers between devices: 416 us -> none  [shards(): draws = lax.all_gather(factor_draws, ('scen', 'obl'), axis=0, tiled=True)]
    dot_general x64 -> x0, matrix products: 265 us -> none  [the longest x32 135 us: grad_step(): lax.dot_general(slope, draw_block, (((0,), (0,)), ((), ())), preferred_el...]
    psum x1 -> x0, waiting for transfers between devices: 239 us -> none  [shards(): cumulant, twisted_loss = lax.psum((cumulant, twisted_loss), ('scen', 'obl'))]
    pallas_call x0 -> x1, Pallas kernels: none -> 78.8 us  [shards(): pl.pallas_call(kernel, out_shape=[jax.ShapeDtypeStruct((1, OWN), F32), ja...]
    mul x97 -> x0, other arithmetic: 42.8 us -> none  [the longest x64 41.9 us: obligor_terms(): denom = 1.0 + prob * (growth - 1.0)]
  transfers between devices with their start and end apart: 2 -> 0, of which waited for: 2 -> 0; matrix products, arithmetic and copies ran while one was open for 0% -> 0% of each run, Pallas kernels for 0% -> 0%
where the time goes in v1:
time: 83 us; the launch traced here: 82.8 us
  Pallas kernels  78.8 us (95%)
  local copies, waits for them, and re-layouts  2.74 us (3%)
  between operations  1.3 us (2%)
    pallas_call x1, Pallas kernels, shards(): pl.pallas_call(kernel, out_shape=[jax.ShapeDtypeStruct((1, OWN), F32), ja...  78.8 us
    unnamed x4, local copies, waits for them, and re-layouts  2.74 us

profile of v1, /device:TPU:1, one launch (start us, length us, event | category | flops | bytes accessed | tf_op | source)
XLA Modules:
  0.0 82.8 jit_solution(14965834621704590671)
XLA Ops:
  1.3 78.8 %shard_map.86 = (f32[1,64]{1,0:T(1,128)}, f32[512,128]{1,0:T(8,128)}) custom-call(bf16[64,128]{1,0:T(8,128)(2,1)} %draws_ref.1, bf16[512,128]{1,0:T(8,128)(2,1)} %load_ref.1, s32[4,128]{1,0:T(4,128)} %bitcast.5, bf16[4,128]{1,0:T(4,128)(2,1)} %bitcast.6, bf16[4,128]{1,0:T(4,128)(2,1)} %bitcast.7, bf16[4,128]{1,0:T(4,128)(2,1)} %bitcast.8, f32[1]{0:T(128)S(6)} %copy.11.theta_ref), custom_call_target="tpu_custom_call" | custom-call | tf_op jit(solution)/shard_map/pallas_call | solution.py:410
  80.1 0.0 copy-start
  80.1 0.6 copy-done
  80.7 0.5 copy.12
  81.2 1.7 %copy.13 = f32[512,128]{1,0:T(8,128)} copy(f32[512,128]{1,0:T(8,128)} %get-tuple-element.9) | data formatting | bytes 524288
Async XLA Ops:
  80.1 0.6 copy-start

commit v2 on v1

--- a/solution.py
+++ b/solution.py
@@ -25,7 +25,12 @@
 ROWS = 128
 GROUP = 64
 STRETCH = 256
+DEEP = 2048
+FULL = 8
+LAST = 2
 PEERS = SIDE * SIDE
+FAR_PLANE = sorted(range(1, PEERS), key=lambda s: -min(s // SIDE, SIDE - s // SIDE) - min(s % SIDE, SIDE - s % SIDE))
+FAR_STACK = sorted(range(1, PEERS), key=lambda s: -min(s // 2, DEPTH - s // 2))
 ROOT_HALF = 0.7071067811865476
 NORMAL_PEAK = 0.3989422804014327
 SCALE_OUT = 300.0
@@ -33,14 +38,22 @@
 NT = (((1,), (1,)), ((), ()))
 
 
+def div(a, b):
+    return lax.div(a, jnp.int32(b))
+
+
+def rem(a, b):
+    return lax.rem(a, jnp.int32(b))
+
+
 def place():
     scen, obl = lax.axis_index("scen"), lax.axis_index("obl")
-    z = (obl // 8) * 2 + scen // 4
-    return (obl // 2) % 4, scen % 4, z, obl % 2
+    z = div(obl, 8) * 2 + div(scen, 4)
+    return rem(div(obl, 2), 4), rem(scen, 4), z, rem(obl, 2)
 
 
 def device(x, y, z, core):
-    return ((z % 2) * 4 + y, (z // 2) * 8 + x * 2 + core)
+    return (rem(z, 2) * 4 + y, div(z, 2) * 8 + x * 2 + core)
 
 
 def columns(row):
@@ -52,17 +65,24 @@
 
 
 def kernel(
-    draws_ref,
+    draws_hbm,
+    load_hbm,
+    sector_hbm,
+    threshold_hbm,
+    idio_hbm,
+    exposure_hbm,
+    theta_ref,
+    weight_ref,
+    sens_ref,
     load_ref,
     sector_ref,
     threshold_ref,
     idio_ref,
     exposure_ref,
-    theta_ref,
-    weight_ref,
-    sens_ref,
+    local,
     draws,
     slopes,
+    kept,
     active,
     inverse,
     offset,
@@ -81,6 +101,8 @@
     recv2,
     send3,
     recv3,
+    send_h,
+    recv_h,
     send_f,
     recv_f,
     send_r,
@@ -91,28 +113,52 @@
     p2 = x + core * (y - x)
 
     def along1(step):
-        q = (p1 + step) % SIDE
+        q = rem(p1 + step, SIDE)
         return device(x + core * (q - x), y + (1 - core) * (q - y), z, core)
 
     def along2(step):
-        q = (p2 + step) % SIDE
+        q = rem(p2 + step, SIDE)
         return device(x + (1 - core) * (q - x), y + core * (q - y), z, core)
 
     partner = device(x, y, z, 1 - core)
     plane = x * SIDE + y
     stack = z * 2 + core
 
+    def plane_to(step):
+        return rem(x + step // SIDE, SIDE) * SIDE + rem(y + step % SIDE, SIDE)
+
+    def plane_from(step):
+        return plane_to((SIDE - step // SIDE) % SIDE * SIDE + (SIDE - step % SIDE) % SIDE)
+
+    def stack_to(step):
+        return rem(z + step // 2, DEPTH) * 2 + rem(core + step % 2, 2)
+
+    def stack_from(step):
+        return stack_to((DEPTH - step // 2) % DEPTH * 2 + step % 2)
+
     def plane_peer(j):
-        return device(j // SIDE, j % SIDE, z, core)
+        return device(div(j, SIDE), rem(j, SIDE), z, core)
 
     def stack_peer(j):
-        return device(x, y, j // 2, j % 2)
+        return device(x, y, div(j, 2), rem(j, 2))
+
+    def fetch(source, target, slot):
+        copy = pltpu.make_async_copy(source, target, local.at[slot])
+        copy.start()
+        return copy
+
+    inputs = [
+        fetch(sector_hbm, sector_ref, 0),
+        fetch(threshold_hbm, threshold_ref, 1),
+        fetch(idio_hbm, idio_ref, 2),
+        fetch(exposure_hbm, exposure_ref, 3),
+        fetch(load_hbm, load_ref, 4),
+    ]
 
     barrier = pltpu.get_barrier_semaphore()
     for step in range(1, PEERS):
-        for peer in (plane_peer((plane + step) % PEERS), stack_peer((stack + step) % PEERS)):
+        for peer in (plane_peer(plane_to(step)), stack_peer(stack_to(step))):
             pl.semaphore_signal(barrier, inc=1, device_id=peer, device_id_type=MESH)
-    pl.semaphore_wait(barrier, 2 * (PEERS - 1))
 
     def unit_index(half, a, b):
         return half * PEERS + a * SIDE + b
@@ -121,19 +167,19 @@
         return pl.ds(pl.multiple_of(index * UNIT, UNIT), UNIT)
 
     def own_index(d, e):
-        return unit_index(core, (p2 + SIDE - d) % SIDE, (p1 + SIDE - e) % SIDE)
+        return unit_index(core, rem(p2 + SIDE - d, SIDE), rem(p1 + SIDE - e, SIDE))
 
     def partner_index(d, e):
-        return unit_index(1 - core, (p1 + SIDE - d) % SIDE, (p2 + SIDE - e) % SIDE)
+        return unit_index(1 - core, rem(p1 + SIDE - d, SIDE), rem(p2 + SIDE - e, SIDE))
 
     def copy1(step, from_z):
         rows = pl.ds(pl.multiple_of(own_index(0, 0) * UNIT + from_z * OWN, OWN), OWN)
         return pltpu.make_async_remote_copy(
-            src_ref=draws_ref,
+            src_ref=draws.at[rows],
             dst_ref=draws.at[rows],
             send_sem=send1.at[step],
             recv_sem=recv1.at[step],
-            device_id=device(x, y, (z + step) % DEPTH, core),
+            device_id=device(x, y, rem(z + step, DEPTH), core),
             device_id_type=MESH,
         )
 
@@ -154,13 +200,37 @@
     def copy3(e, step, d):
         return unit_copy(own_index(d, e), send3.at[e, step], recv3.at[e, step], along2(step))
 
+    def relay(e, half):
+        d, step = 1 + 2 * half, 1 + 2 * half
+        rows = pl.ds(pl.multiple_of(own_index(d, e) * UNIT + half * (UNIT // 2), UNIT // 2), UNIT // 2)
+        return relay_copy(rows, e, half, along2(step))
+
+    def relayed(e, half):
+        rows = pl.ds(pl.multiple_of(own_index(2, e) * UNIT + half * (UNIT // 2), UNIT // 2), UNIT // 2)
+        return relay_copy(rows, e, half, along2(1 + 2 * half))
+
+    def relay_copy(rows, e, half, peer):
+        return pltpu.make_async_remote_copy(
+            src_ref=draws.at[rows],
+            dst_ref=draws.at[rows],
+            send_sem=send_h.at[e, half],
+            recv_sem=recv_h.at[e, half],
+            device_id=peer,
+            device_id_type=MESH,
+        )
+
     def forward(d, e, index):
         return unit_copy(index, send_f.at[d, e], recv_f.at[d, e], partner)
 
-    for step in range(1, DEPTH):
+    mine = pl.ds(pl.multiple_of(own_index(0, 0) * UNIT + z * OWN, OWN), OWN)
+    own_draws = fetch(draws_hbm, draws.at[mine], 5)
+    own_draws.wait()
+    pl.semaphore_wait(barrier, 2 * (PEERS - 1))
+    for step in (4, 3, 5, 2, 6, 1, 7):
         copy1(step, z).start()
-    mine = pl.ds(pl.multiple_of(own_index(0, 0) * UNIT + z * OWN, OWN), OWN)
-    draws[mine, :] = draws_ref[...]
+
+    for copy in inputs:
+        copy.wait()
 
     twist = theta_ref[0]
     ids = lax.broadcasted_iota(jnp.int32, (LANES, FACTORS), 1)
@@ -202,7 +272,7 @@
         active[rows, :] = jnp.where(mask, load_ref[rows, :].astype(F32), 0.0).astype(BF16)
         scale[rows, :] = jnp.where(mask, scale[rows, :], 0.0)
 
-    def compute(index):
+    def compute(index, slot, logits, steep):
         draw_rows = draws[unit_rows(index), :]
         lanes = pl.ds(pl.multiple_of(index * UNIT, UNIT), UNIT)
         acc = jnp.zeros((8, UNIT), F32)
@@ -211,9 +281,17 @@
             rows = pl.ds(r, ROWS)
             score = lax.dot_general(active[rows, :], draw_rows, NT, preferred_element_type=F32)
             arg = score * wide(inverse[rows, :]) + wide(offset[rows, :])
-            denom = lax.erf(arg) + wide(shift[rows, :])
-            share = pl.reciprocal(denom)
-            slopes[rows, lanes] = (jnp.exp2((arg * arg) * -LOG2_E) * share * share).astype(BF16)
+            if logits:
+                denom = lax.erf(arg) + wide(shift[rows, :])
+                share = pltpu.reciprocal(denom)
+                if not steep:
+                    kept[slot, rows, :] = share
+            else:
+                share = kept[slot, rows, :]
+            if steep:
+                slopes[rows, lanes] = (jnp.exp2((arg * arg) * -LOG2_E) * share * share).astype(BF16)
+            if not logits:
+                continue
             loss = share * wide(gain[rows, :])
             if r % STRETCH == 0:
                 product = denom[:8]
@@ -226,48 +304,99 @@
                 acc = acc + (some - wide(centre[pl.ds((r + g) // GROUP * 8, 8), :]))
             if (r + ROWS) % STRETCH == 0:
                 acc = acc + jnp.log(product * wide(level[pl.ds(r // STRETCH * 8, 8), :]))
-        logit[pl.ds(index, 1), :] = jnp.sum(acc, axis=0, keepdims=True)
+        if logits:
+            logit[pl.ds(index, 1), :] = jnp.sum(acc, axis=0, keepdims=True)
 
     for step in range(1, DEPTH):
-        copy1(step, (z + DEPTH - step) % DEPTH).wait_recv()
-    for step in range(1, SIDE):
+        copy1(step, rem(z + DEPTH - step, DEPTH)).wait_recv()
+    for step in (1, 3, 2):
         copy2(step, 0).start()
 
-    def turn(n, carry):
-        group, e = n // SIDE, n % SIDE
-        d = group + (group // 2) * (5 - 2 * group)
-
-        @pl.when((n > 0) & (n < SIDE))
+    def swap(i):
+        return i + 1 + rem(i, 2) - div(i, 2)
+
+    def order(n):
+        early = swap(jnp.minimum(div(jnp.maximum(n - 1, 0), 2), 2))
+        odd = rem(n, 2)
+        late = jnp.maximum(n - 6, 0)
+        g, i = div(late, 3), rem(late, 3)
+        before = jnp.where(g == 0, 0, swap(jnp.maximum(g - 1, 0)))
+        d = jnp.where(n < 6, jnp.where((n > 0) & (odd == 0), early, 0), jnp.where((i == 2) | (g == 3), 2, 1 + 2 * i))
+        e = jnp.where(n < 6, jnp.where(odd == 1, early, 0), jnp.where((i == 2) | (g == 3), before, swap(jnp.minimum(g, 2))))
+        return d, e
+
+    def unit_of(k):
+        mine = (k == 0) | (k == 2) | ((rem(k, 2) == 1) & (k > 2) & (k < UNITS - 1))
+        n = jnp.where(mine, div(k + 1, 2), jnp.where(k == UNITS - 1, UNITS // 2 - 1, div(k, 2) - (k > 1)))
+        d, e = order(n)
+        return mine, d, e, jnp.where(mine, own_index(d, e), partner_index(d, e))
+
+    def arrive(k):
+        mine, d, e, index = unit_of(k)
+
+        @pl.when(mine)
         def _():
-            copy2(e, e).wait_recv()
-
-        @pl.when(n >= SIDE)
+            @pl.when((d == 0) & (e > 0))
+            def _():
+                copy2(e, e).wait_recv()
+
+            direct = (d == 1) | (d == 3) | ((d == 2) & (e == LAST))
+
+            @pl.when(direct)
+            def _():
+                copy3(e, d, d).wait_recv()
+
+            @pl.when((d == 2) & (e != LAST))
+            def _():
+                for half in range(2):
+                    relayed(e, half).wait_recv()
+
+            @pl.when(d == 0)
+            def _():
+                for step in (1, 3):
+                    copy3(e, step, 0).start()
+
+            forward(d, e, own_index(d, e)).start()
+
+            @pl.when((d == 0) & (e == LAST))
+            def _():
+                copy3(e, 2, 0).start()
+
+            for half in range(2):
+
+                @pl.when((d == 1 + 2 * half) & (e != LAST))
+                def _():
+                    relay(e, half).start()
+
+        @pl.when(jnp.logical_not(mine))
         def _():
-            copy3(e, d, d).wait_recv()
-
-        @pl.when(n < SIDE)
-        def _():
-            for step in range(1, SIDE):
-                copy3(e, step, 0).start()
-
-        forward(d, e, own_index(d, e)).start()
-
-        def side(which, carry):
-            @pl.when(which == 1)
-            def _():
-                forward(d, e, partner_index(d, e)).wait_recv()
-
-            compute(own_index(d, e) + which * (partner_index(d, e) - own_index(d, e)))
+            forward(d, e, partner_index(d, e)).wait_recv()
+
+        return index
+
+    def turn(steep, pair, carry):
+        first, second = arrive(2 * pair), arrive(2 * pair + 1)
+        compute(first, 2 * pair - FULL, True, steep)
+        compute(second, 2 * pair + 1 - FULL, True, steep)
+        return carry
+
+    lax.fori_loop(0, FULL // 2, functools.partial(turn, True), 0)
+    lax.fori_loop(FULL // 2, UNITS // 2, functools.partial(turn, False), 0)
+
+    def late_slopes(part):
+        def two(pair, carry):
+            indices = [unit_of(2 * pair + i)[3] for i in range(2)]
+            for i in range(2):
+                compute(indices[i], 2 * pair + i - FULL, False, True)
             return carry
 
-        return lax.fori_loop(0, 2, side, carry)
-
-    lax.fori_loop(0, UNITS // 2, turn, 0)
+        third = (UNITS - FULL) // 6
+        lax.fori_loop(FULL // 2 + part * third, FULL // 2 + (part + 1) * third, two, 0)
 
     def tile(j):
         return (
-            pl.ds(pl.multiple_of(j // SIDE * 8, 8), 8),
-            pl.ds(pl.multiple_of(j % SIDE * LANES, LANES), LANES),
+            pl.ds(pl.multiple_of(div(j, SIDE) * 8, 8), 8),
+            pl.ds(pl.multiple_of(rem(j, SIDE) * LANES, LANES), LANES),
         )
 
     def reduce1(step, j, peer):
@@ -301,7 +430,7 @@
         )
 
     def arrival1(step):
-        j = (plane + PEERS - step) % PEERS
+        j = plane_from(step)
         return pltpu.make_async_remote_copy(
             src_ref=logit.at[tile(plane)],
             dst_ref=part1.at[j],
@@ -312,7 +441,7 @@
         )
 
     def arrival2(step):
-        j = (stack + PEERS - step) % PEERS
+        j = stack_from(step)
         return pltpu.make_async_remote_copy(
             src_ref=part2.at[stack],
             dst_ref=part2.at[j],
@@ -323,7 +452,7 @@
         )
 
     def arrival3(step):
-        j = (plane + PEERS - step) % PEERS
+        j = plane_from(step)
         return pltpu.make_async_remote_copy(
             src_ref=total.at[tile(plane)],
             dst_ref=total.at[tile(j)],
@@ -334,35 +463,42 @@
         )
 
     def to_plane(step):
-        j = (plane + step) % PEERS
+        j = plane_to(step)
         return reduce1(step, j, plane_peer(j))
 
     def to_stack(step):
-        return reduce2(step, stack_peer((stack + step) % PEERS))
+        return reduce2(step, stack_peer(stack_to(step)))
 
     def back_to_plane(step):
-        return reduce3(step, plane_peer((plane + step) % PEERS))
-
-    for step in range(1, PEERS):
+        return reduce3(step, plane_peer(plane_to(step)))
+
+    for step in FAR_PLANE:
         to_plane(step).start()
     part1[plane] = logit[tile(plane)]
+    late_slopes(0)
     for step in range(1, PEERS):
         arrival1(step).wait_recv()
     part2[stack] = jnp.sum(part1[...], axis=0)
-    for step in range(1, PEERS):
+    for step in FAR_STACK:
         to_stack(step).start()
+    late_slopes(1)
     for step in range(1, PEERS):
         arrival2(step).wait_recv()
     total[tile(plane)] = jnp.sum(part2[...], axis=0)
-    for step in range(1, PEERS):
+    for step in FAR_PLANE:
         back_to_plane(step).start()
-
+    late_slopes(2)
     for step in range(1, DEPTH):
         copy1(step, z).wait_send()
     for step in range(1, SIDE):
         copy2(step, 0).wait_send()
         for e in range(SIDE):
-            copy3(e, step, 0).wait_send()
+            if step != 2 or e == LAST:
+                copy3(e, step, 0).wait_send()
+    for e in range(SIDE):
+        for half in range(2):
+            if e != LAST:
+                relay(e, half).wait_send()
     for d in range(SIDE):
         for e in range(SIDE):
             forward(d, e, own_index(d, e)).wait_send()
@@ -384,21 +520,17 @@
         own = jnp.where(z == k, own_row[:, k * OWN : (k + 1) * OWN], own)
     weight_ref[...] = own * (norm * SCENARIOS)
 
-    for j in range(UNIT // LANES):
-        turned = jnp.transpose(raw[:, j * LANES : (j + 1) * LANES])
-        for u in range(UNITS):
-            rows = pl.ds(u * UNIT + j * LANES, LANES)
-            draws[rows, :] = (draws[rows, :].astype(F32) * turned[:, u : u + 1]).astype(BF16)
-
     sens_ref[...] = jnp.zeros_like(sens_ref)
-    depth = 2 * UNIT
 
     def add(n, carry):
-        at = pl.ds(pl.multiple_of(n * depth, depth), depth)
-        sens_ref[...] += jnp.dot(slopes[:, at], draws[at, :], preferred_element_type=F32)
+        at = pl.ds(pl.multiple_of(n * DEEP, DEEP), DEEP)
+        rows = [total[pl.ds(n * (DEEP // UNIT) + k, 1), :] for k in range(DEEP // UNIT)]
+        row = jnp.broadcast_to(jnp.concatenate(rows, axis=1), (16, DEEP)).astype(BF16)
+        weighted = slopes[:, at] * jnp.concatenate([row] * (OBL // 16), axis=0)
+        sens_ref[...] += jnp.dot(weighted, draws[at, :], preferred_element_type=F32)
         return carry
 
-    lax.fori_loop(0, SCENARIOS // depth, add, 0)
+    lax.fori_loop(0, SCENARIOS // DEEP, add, 0)
     sens_ref[...] = sens_ref[...] * (scale[...] * norm)
 
 
@@ -413,11 +545,18 @@
             jax.ShapeDtypeStruct((1, OWN), F32),
             jax.ShapeDtypeStruct((OBL, FACTORS), F32),
         ],
-        in_specs=[vmem] * 6 + [pl.BlockSpec(memory_space=pltpu.SMEM)],
+        in_specs=[pl.BlockSpec(memory_space=pl.ANY)] * 6 + [pl.BlockSpec(memory_space=pltpu.SMEM)],
         out_specs=[vmem] * 2,
         scratch_shapes=[
+            pltpu.VMEM((OBL, FACTORS), BF16),
+            pltpu.VMEM((rows, LANES), jnp.int32),
+            pltpu.VMEM((rows, LANES), BF16),
+            pltpu.VMEM((rows, LANES), BF16),
+            pltpu.VMEM((rows, LANES), BF16),
+            dma((6,)),
             pltpu.VMEM((SCENARIOS, FACTORS), BF16),
             pltpu.VMEM((OBL, SCENARIOS), BF16),
+            pltpu.VMEM((UNITS - FULL, OBL, UNIT), F32),
             pltpu.VMEM((OBL, FACTORS), BF16),
             constant,
             constant,
@@ -436,13 +575,15 @@
             dma((SIDE,)),
             dma((SIDE, SIDE)),
             dma((SIDE, SIDE)),
+            dma((SIDE, 2)),
+            dma((SIDE, 2)),
             dma((SIDE, SIDE)),
             dma((SIDE, SIDE)),
             dma((3, PEERS)),
             dma((3, PEERS)),
         ],
         compiler_params=pltpu.CompilerParams(
-            collective_id=0, has_side_effects=True, vmem_limit_bytes=56 << 20
+            collective_id=0, has_side_effects=True, vmem_limit_bytes=58 << 20
         ),
     )(
         factor_draws,

time: 83 us -> 64.3 us (0.77)
  Pallas kernels: 78.8 us -> 60.1 us
    pallas_call x1, Pallas kernels: 78.8 us -> 60.1 us  [shards(): pl.pallas_call(kernel, out_shape=[jax.ShapeDtypeStruct((1, OWN), F32), ja...]
where the time goes in v2:
time: 64.3 us; the launch traced here: 64.1 us
  Pallas kernels  60.1 us (93%)
  local copies, waits for them, and re-layouts  2.74 us (4%)
  between operations  1.3 us (2%)
    pallas_call x1, Pallas kernels, shards(): pl.pallas_call(kernel, out_shape=[jax.ShapeDtypeStruct((1, OWN), F32), ja...  60.1 us
    unnamed x4, local copies, waits for them, and re-layouts  2.74 us

profile of v2, /device:TPU:1, one launch (start us, length us, event | category | flops | bytes accessed | tf_op | source)
XLA Modules:
  0.0 64.1 jit_solution(5341613695938342804)
XLA Ops:
  1.3 60.1 %shard_map.86 = (f32[1,64]{1,0:T(1,128)}, f32[512,128]{1,0:T(8,128)}) custom-call(bf16[64,128]{1,0:T(8,128)(2,1)} %draws_hbm.1, bf16[512,128]{1,0:T(8,128)(2,1)} %load_hbm.1, s32[4,128]{1,0:T(4,128)} %bitcast.5, bf16[4,128]{1,0:T(4,128)(2,1)} %bitcast.6, bf16[4,128]{1,0:T(4,128)(2,1)} %bitcast.7, bf16[4,128]{1,0:T(4,128)(2,1)} %bitcast.8, f32[1]{0:T(128)S(6)} %copy.11.theta_ref), custom_call_target="tpu_custom_call" | custom-call | tf_op jit(solution)/shard_map/pallas_call | solution.py:542
  61.3 0.0 copy-start
  61.4 0.6 copy-done
  61.9 0.5 copy.12
  62.4 1.7 %copy.13 = f32[512,128]{1,0:T(8,128)} copy(f32[512,128]{1,0:T(8,128)} %get-tuple-element.9) | data formatting | bytes 524288
Async XLA Ops:
  61.3 0.6 copy-start

commit v3 on v2

--- a/solution.py
+++ b/solution.py
@@ -25,9 +25,8 @@
 ROWS = 128
 GROUP = 64
 STRETCH = 256
-DEEP = 2048
+DEEP = 4096
 FULL = 8
-LAST = 2
 PEERS = SIDE * SIDE
 FAR_PLANE = sorted(range(1, PEERS), key=lambda s: -min(s // SIDE, SIDE - s // SIDE) - min(s % SIDE, SIDE - s % SIDE))
 FAR_STACK = sorted(range(1, PEERS), key=lambda s: -min(s // 2, DEPTH - s // 2))
@@ -101,8 +100,6 @@
     recv2,
     send3,
     recv3,
-    send_h,
-    recv_h,
     send_f,
     recv_f,
     send_r,
@@ -199,25 +196,6 @@
 
     def copy3(e, step, d):
         return unit_copy(own_index(d, e), send3.at[e, step], recv3.at[e, step], along2(step))
-
-    def relay(e, half):
-        d, step = 1 + 2 * half, 1 + 2 * half
-        rows = pl.ds(pl.multiple_of(own_index(d, e) * UNIT + half * (UNIT // 2), UNIT // 2), UNIT // 2)
-        return relay_copy(rows, e, half, along2(step))
-
-    def relayed(e, half):
-        rows = pl.ds(pl.multiple_of(own_index(2, e) * UNIT + half * (UNIT // 2), UNIT // 2), UNIT // 2)
-        return relay_copy(rows, e, half, along2(1 + 2 * half))
-
-    def relay_copy(rows, e, half, peer):
-        return pltpu.make_async_remote_copy(
-            src_ref=draws.at[rows],
-            dst_ref=draws.at[rows],
-            send_sem=send_h.at[e, half],
-            recv_sem=recv_h.at[e, half],
-            device_id=peer,
-            device_id_type=MESH,
-        )
 
     def forward(d, e, index):
         return unit_copy(index, send_f.at[d, e], recv_f.at[d, e], partner)
@@ -317,12 +295,12 @@
 
     def order(n):
         early = swap(jnp.minimum(div(jnp.maximum(n - 1, 0), 2), 2))
-        odd = rem(n, 2)
+        odd = jnp.where(n == 5, 0, rem(n, 2))
         late = jnp.maximum(n - 6, 0)
         g, i = div(late, 3), rem(late, 3)
         before = jnp.where(g == 0, 0, swap(jnp.maximum(g - 1, 0)))
-        d = jnp.where(n < 6, jnp.where((n > 0) & (odd == 0), early, 0), jnp.where((i == 2) | (g == 3), 2, 1 + 2 * i))
-        e = jnp.where(n < 6, jnp.where(odd == 1, early, 0), jnp.where((i == 2) | (g == 3), before, swap(jnp.minimum(g, 2))))
+        d = jnp.where(n < 6, jnp.where(odd == 1, early, 0), jnp.where((i == 2) | (g == 3), 2, 1 + 2 * i))
+        e = jnp.where(n < 6, jnp.where((n > 0) & (odd == 0), early, 0), jnp.where((i == 2) | (g == 3), before, swap(jnp.minimum(g, 2))))
         return d, e
 
     def unit_of(k):
@@ -340,16 +318,9 @@
             def _():
                 copy2(e, e).wait_recv()
 
-            direct = (d == 1) | (d == 3) | ((d == 2) & (e == LAST))
-
-            @pl.when(direct)
+            @pl.when(d > 0)
             def _():
                 copy3(e, d, d).wait_recv()
-
-            @pl.when((d == 2) & (e != LAST))
-            def _():
-                for half in range(2):
-                    relayed(e, half).wait_recv()
 
             @pl.when(d == 0)
             def _():
@@ -358,15 +329,9 @@
 
             forward(d, e, own_index(d, e)).start()
 
-            @pl.when((d == 0) & (e == LAST))
+            @pl.when(d == 0)
             def _():
                 copy3(e, 2, 0).start()
-
-            for half in range(2):
-
-                @pl.when((d == 1 + 2 * half) & (e != LAST))
-                def _():
-                    relay(e, half).start()
 
         @pl.when(jnp.logical_not(mine))
         def _():
@@ -493,12 +458,7 @@
     for step in range(1, SIDE):
         copy2(step, 0).wait_send()
         for e in range(SIDE):
-            if step != 2 or e == LAST:
-                copy3(e, step, 0).wait_send()
-    for e in range(SIDE):
-        for half in range(2):
-            if e != LAST:
-                relay(e, half).wait_send()
+            copy3(e, step, 0).wait_send()
     for d in range(SIDE):
         for e in range(SIDE):
             forward(d, e, own_index(d, e)).wait_send()
@@ -575,8 +535,6 @@
             dma((SIDE,)),
             dma((SIDE, SIDE)),
             dma((SIDE, SIDE)),
-            dma((SIDE, 2)),
-            dma((SIDE, 2)),
             dma((SIDE, SIDE)),
             dma((SIDE, SIDE)),
             dma((3, PEERS)),

time: 64.3 us -> 62.6 us (0.974)
  Pallas kernels: 60.1 us -> 58.3 us
    pallas_call x1, Pallas kernels: 60.1 us -> 58.3 us  [shards(): pl.pallas_call(kernel, out_shape=[jax.ShapeDtypeStruct((1, OWN), F32), ja...]
where the time goes in v3:
time: 62.6 us; the launch traced here: 62.4 us
  Pallas kernels  58.3 us (93%)
  local copies, waits for them, and re-layouts  2.74 us (4%)
  between operations  1.3 us (2%)
    pallas_call x1, Pallas kernels, shards(): pl.pallas_call(kernel, out_shape=[jax.ShapeDtypeStruct((1, OWN), F32), ja...  58.3 us
    unnamed x4, local copies, waits for them, and re-layouts  2.74 us

profile of v3, /device:TPU:1, one launch (start us, length us, event | category | flops | bytes accessed | tf_op | source)
XLA Modules:
  0.0 62.4 jit_solution(5545536720571339721)
XLA Ops:
  1.3 58.3 %shard_map.86 = (f32[1,64]{1,0:T(1,128)}, f32[512,128]{1,0:T(8,128)}) custom-call(bf16[64,128]{1,0:T(8,128)(2,1)} %draws_hbm.1, bf16[512,128]{1,0:T(8,128)(2,1)} %load_hbm.1, s32[4,128]{1,0:T(4,128)} %bitcast.5, bf16[4,128]{1,0:T(4,128)(2,1)} %bitcast.6, bf16[4,128]{1,0:T(4,128)(2,1)} %bitcast.7, bf16[4,128]{1,0:T(4,128)(2,1)} %bitcast.8, f32[1]{0:T(128)S(6)} %copy.11.theta_ref), custom_call_target="tpu_custom_call" | custom-call | tf_op jit(solution)/shard_map/pallas_call | solution.py:502
  59.6 0.0 copy-start
  59.6 0.6 copy-done
  60.2 0.5 copy.12
  60.7 1.7 %copy.13 = f32[512,128]{1,0:T(8,128)} copy(f32[512,128]{1,0:T(8,128)} %get-tuple-element.9) | data formatting | bytes 524288
Async XLA Ops:
  59.6 0.6 copy-start
